TPU v7x, 32 devices: a whole 2x2x4 slice. The times are simulated.
32 devices in a mesh: plans: 2 (over y), vox: 8 (over z, x), beam: 2 (over core).
Axes of the slice: x: 2, y: 2, z: 4, core: 2. Of those that a mesh axis runs over, the one named last changes fastest.
Arguments:
- fluence: float32 [16, 2, 16384], P('plans', 'beam', 'vox'), parts along dimension 0, may hold values from 0 to 1
- tile_values: float32 [16, 2, 32, 128, 128], P(('plans', 'vox'), 'beam'), parts along dimension 0, may hold values from 0 to 0.015625
- tile_rows: int32 [16, 2, 32], P(('plans', 'vox'), 'beam'), parts along dimension 0, may hold values from 0 to 31, as said below
- tile_columns: int32 [16, 2, 32], P(('plans', 'vox'), 'beam'), parts along dimension 0, may hold values from 0 to 127, as said below
- tile_count: int32 [16, 2], P(('plans', 'vox'), 'beam'), parts along dimension 0, may hold values from 1 to 32, as said below
- labels: int32 [65536], P(('plans', 'vox')), parts along dimension 0, may hold values from 0 to 3
- prescribed: float32 [8], P('plans'), parts along dimension 0, may hold values from 0.2 to 1
- weights: float32 [16, 4], P('plans'), parts along dimension 0, may hold values from 0.5 to 4
- smoothing: float32 [16], P('plans'), parts along dimension 0, may hold values from 0.2 to 2
- beam_neighbours: int32 [128, 3], P('plans'), parts along dimension 0, may hold values from 0 to 63, as said below
Outputs:
- dose_field: float32 [16, 32768], P('plans', 'vox'), parts along dimension 0
- gradient: float32 [16, 2, 16384], P('plans', 'beam', 'vox'), parts along dimension 0
There are 2 independent parts, one for each index of `plans`. A program takes and returns all parts, laid end to end along the dimension named above; each array names one. Nothing has to cross between parts.
Inputs may be any that keep to these rules, and one draw needn't show every extreme that they name: The pairs (tile_rows, tile_columns) of one device's 32 slots are distinct; entries of slots at or after that device's tile_count are ignored. `tile_columns`: see tile_rows. `tile_count`: uneven over devices; some device uses all 32 slots. `beam_neighbours`: every beam appears as some beam's neighbour.
All inputs are finite; a program needn't handle non-finite values.
Results may differ from a plain program's by a relative error of at most 0.0003.
Values sent between devices are 32-bit elements; how exact they have to be, the bound alone decides.
A program may use at most 64 MiB of HBM per device.

v0:
```python
import jax
import jax.numpy as jnp
from jax import lax
from jax.sharding import PartitionSpec as P

TILE = 128
BLB = 512


highest = lax.Precision.HIGHEST


def penalty_residual(dose, labels, prescribed, weights):
    target = jnp.zeros(dose.shape[1:], jnp.float32)
    scaled = jnp.zeros(dose.shape, jnp.float32)
    for structure in range(prescribed.shape[0]):
        member = labels == structure
        target = jnp.where(member, prescribed[structure], target)
        scaled = jnp.where(member[None, :], weights[:, structure : structure + 1], scaled)
    excess = dose - target[None, :]
    excess = jnp.where(labels[None, :] == 0, excess, jnp.maximum(excess, 0.0))
    return scaled * excess


def forward_tiles(values, row_list, column_list, in_use, fluence_blocks, row_blocks, width):
    weight_count = fluence_blocks.shape[0]
    turns = (in_use + width - 1) // width

    def forward_one_turn(turn, total):
        first = turn * width
        tiles = lax.dynamic_slice_in_dim(values, first, width, 0)
        row_part = lax.dynamic_slice_in_dim(row_list, first, width, 0)
        column_part = lax.dynamic_slice_in_dim(column_list, first, width, 0)
        active = first + jnp.arange(width) < in_use
        picked = jnp.take(fluence_blocks, column_part, axis=1)
        product = jnp.einsum("kst,sut->ksu", picked, tiles, precision=highest)
        place = jnp.where(
            (row_part[None, :] == jnp.arange(row_blocks)[:, None]) & active[None, :], 1.0, 0.0
        ).astype(jnp.float32)
        return total + jnp.einsum("rs,ksu->kru", place, product, precision=highest)

    start_total = jnp.zeros((weight_count, row_blocks, TILE), jnp.float32)
    return lax.fori_loop(0, turns, forward_one_turn, start_total)


def adjoint_tiles(values, row_list, column_list, in_use, residual_blocks, column_blocks, width):
    weight_count = residual_blocks.shape[0]
    turns = (in_use + width - 1) // width

    def adjoint_one_turn(turn, total):
        first = turn * width
        tiles = lax.dynamic_slice_in_dim(values, first, width, 0)
        row_part = lax.dynamic_slice_in_dim(row_list, first, width, 0)
        column_part = lax.dynamic_slice_in_dim(column_list, first, width, 0)
        active = first + jnp.arange(width) < in_use
        picked = jnp.take(residual_blocks, row_part, axis=1)
        product = jnp.einsum("ksu,sut->kst", picked, tiles, precision=highest)
        place = jnp.where(
            (column_part[None, :] == jnp.arange(column_blocks)[:, None]) & active[None, :], 1.0, 0.0
        ).astype(jnp.float32)
        return total + jnp.einsum("cs,kst->kct", place, product, precision=highest)

    start_total = jnp.zeros((weight_count, column_blocks, TILE), jnp.float32)
    return lax.fori_loop(0, turns, adjoint_one_turn, start_total)


def local(
    fluence,
    tile_values,
    tile_rows,
    tile_columns,
    tile_count,
    labels,
    prescribed,
    weights,
    smoothing,
    beam_neighbours,
):
    groups = lax.axis_size("beam")
    voxel_parts = lax.axis_size("vox")
    group_index = lax.axis_index("beam")
    voxel_index = lax.axis_index("vox")
    weight_count = fluence.shape[0]
    shard = fluence.shape[2]
    group_width = shard * voxel_parts
    column_blocks = group_width // TILE
    row_blocks = labels.shape[0] // TILE
    own_group = lax.all_gather(fluence, "vox", axis=2, tiled=True)
    everything = lax.all_gather(own_group, "beam", axis=1, tiled=True)
    group_fluence = own_group[:, 0, :]
    fluence_blocks = group_fluence.reshape(weight_count, column_blocks, TILE)
    values = tile_values[0, 0]
    row_list = tile_rows[0, 0]
    column_list = tile_columns[0, 0]
    in_use = tile_count[0, 0]
    capacity = values.shape[0]
    half = capacity // 2
    width = min(8, half)
    partial_value = forward_tiles(
        values, row_list, column_list, in_use, fluence_blocks, row_blocks, width
    )
    dose_blocks = lax.psum(partial_value, "beam")
    dose_out = dose_blocks.reshape(weight_count, row_blocks * TILE)
    residual = penalty_residual(dose_out, labels, prescribed, weights)
    residual_blocks = residual.reshape(weight_count, row_blocks, TILE)
    term = adjoint_tiles(
        values, row_list, column_list, in_use, residual_blocks, column_blocks, width
    )
    adjoint = lax.psum_scatter(
        term.reshape(weight_count, group_width), "vox", scatter_dimension=1, tiled=True
    )
    beam_count = groups * group_width // BLB
    beam_view = everything.reshape(weight_count, beam_count, BLB)
    start = group_index * group_width + voxel_index * shard
    first_beam = start // BLB
    beams_here = max(1, shard // BLB)
    neighbour_rows = lax.dynamic_slice_in_dim(beam_neighbours, first_beam, beams_here, 0)
    around_beams = jnp.zeros((weight_count, beams_here, BLB), jnp.float32)
    for neighbour in range(beam_neighbours.shape[1]):
        around_beams = around_beams + jnp.take(beam_view, neighbour_rows[:, neighbour], axis=1)
    if shard >= BLB:
        beside_all = around_beams.reshape(weight_count, shard)
    else:
        beside_all = lax.dynamic_slice_in_dim(around_beams[:, 0, :], start % BLB, shard, 1)
    spread = beam_neighbours.shape[1] * fluence[:, 0, :] - beside_all
    gradient = adjoint + smoothing[:, None] * spread
    return (dose_out, gradient.reshape(weight_count, 1, shard))


def solution(mesh):
    return jax.shard_map(
        local,
        mesh=mesh,
        in_specs=(
            P("plans", "beam", "vox"),
            P(("plans", "vox"), "beam", None, None, None),
            P(("plans", "vox"), "beam", None),
            P(("plans", "vox"), "beam", None),
            P(("plans", "vox"), "beam"),
            P(("plans", "vox")),
            P("plans"),
            P("plans", None),
            P("plans"),
            P("plans", None),
        ),
        out_specs=(P("plans", "vox"), P("plans", "beam", "vox")),
        check_vma=False,
    )
```

profile of v0, /device:TPU:1, one launch (start us, length us, event | category | flops | bytes accessed | tf_op | source)
XLA Modules:
  0.0 173.7 jit_solution(3326764277169602702)
XLA Ops:
  7.9 0.9 copy.30
  8.8 27.0 %all_gather.6 = f32[8,1,16384]{2,0,1:T(8,128)S(1)} all-gather(f32[8,1,2048]{2,0,1:T(8,128)S(1)} %copy.30), channel_id=1, replica_groups=mesh['plans'=2,'vox'=8,'beam'=2] {'vox'}, dimensions={2}, use_global_device_ids=true | all-gather | bytes 589824 | tf_op jit(solution)/shard_map/all_gather | solution.py:88
  35.8 5.1 %while.20 = (s32[]{:T(128)}, f32[8,32,128]{2,1,0:T(8,128)S(1)}, s32[]{:T(128)}, f32[32,128,128]{2,1,0:T(8,128)}, s32[32]{0:T(128)}, /*index=5*/f32[8,128,128]{2,...) while((s32[]{:T(128)}, f32[8,32,128]{2,1,0:T(8,128)S(1)}, ...), condition=%wide.region_1.2_spmd, body=%wide.region_0.1_spmd.sunk | while | flops 15771462 | bytes 954807 | solution.py:43
  35.8 0.7 dynamic_slice.36
  36.5 1.4 compare_and_fusion.7
  38.5 2.0 %convolution_bitcast_fusion.6 = f32[8,8,128]{2,0,1:T(8,128)S(1)} fusion(f32[32,128,128]{2,1,0:T(8,128)} %get-tuple-element.317, s32[]{:T(128)S(6)} %select_n.164, f32[8,8,128]{2,1,0:T(8,128)S(1)} %gather_fusion, pred[8]{0:T(512)(128)(4,1)S(1)} %get-tuple-element.277), kind=kOutput, calls=%fused_computation.7.clone.1 | convolution fusion | flops 12591104 | bytes 589836 | tf_op jit(solution)/shard_map/while/body/kst,sut->ksu/dot_general | solution.py:36
  40.9 0.8 copy.33
  41.8 0.7 all-gather.2.cloned.1.call-update
  43.2 2.5 %select_bitcast_fusion = (f32[32,128]{1,0:T(8,128)S(1)}, pred[4096]{0:T(1024)(128)(4,1)S(1)}, pred[4096]{0:T(1024)(128)(4,1)S(1)}, pred[4096]{0:T(1024)(128)(4,1)S(1)}, pred[4096]{0:T(1024)(128)(4,1)S(1)}) fusion(f32[]{:T(128)} %bitcast.25, f32[]{:T(128)} %bitcast.24, f32[]{:T(128)} %bitcast.23, f32[]{:T(128)} %bitcast.22, s32[4096]{0:T(1024)S(1)} %copy-done.4), kind=kLoop, calls=%fused_computation.62 | loop fusion | flops 32768 | bytes 49168 | tf_op jit(solution)/shard_map/sub | solution.py:20
  45.7 35.4 %all-reduce.2.cloned.1.call-done = f32[8,32,128]{2,0,1:T(8,128)} async-done(((f32[8,32,128]{2,0,1:T(8,128)}), f32[8,32,128]{2,0,1:T(8,128)}) %all-reduce.2.cloned.1.call-update) | async-done | bytes 131088 | tf_op jit(solution)/shard_map/psum | solution.py:102
  81.2 1.0 fusion.38
  82.3 5.4 %while.21 = (s32[]{:T(128)}, f32[8,128,128]{1,2,0:T(8,128)S(1)}, s32[]{:T(128)}, f32[32,128,128]{2,1,0:T(8,128)}, s32[32]{0:T(128)}, /*index=5*/f32[8,32,128]{2,...) while((s32[]{:T(128)}, f32[8,128,128]{1,2,0:T(8,128)S(1)}, ...), condition=%wide.region_4.5_spmd, body=%wide.region_3.4_spmd.sunk | while | flops 25309252 | bytes 1741239 | solution.py:64
  82.3 0.7 dynamic_slice.38
  83.0 1.4 compare_and_fusion.8
  85.0 1.6 convolution_bitcast_fusion.7
  86.6 1.1 fusion.61
  87.7 1.0 copy.34
  88.9 4.1 %all-gather.2.cloned.1.call-done = f32[8,2,16384]{2,0,1:T(8,128)} async-done(((f32[8,1,16384]{2,0,1:T(8,128)}), f32[8,2,16384]{2,0,1:T(8,128)}) %all-gather.2.cloned.1.call-update) | async-done | bytes 1048592 | tf_op jit(solution)/shard_map/all_gather | solution.py:89
  93.0 1.8 %gather_fusion.4 = f32[4,8,512]{2,1,0:T(8,128)S(1)} fusion(f32[8,64,512]{2,0,1:T(8,128)} %bitcast.99, s32[1024]{0:T(1024)S(1)} %get-tuple-element.176), kind=kCustom, calls=%fused_computation.4.clone | custom fusion | bytes 131088 | tf_op jit(solution)/shard_map/jit(_take)/gather | solution.py:120
  94.8 1.8 %gather_fusion.3 = f32[4,8,512]{2,1,0:T(8,128)S(1)} fusion(f32[8,64,512]{2,0,1:T(8,128)} %bitcast.100, s32[1024]{0:T(1024)S(1)} %get-tuple-element.177), kind=kCustom, calls=%fused_computation.3.clone | custom fusion | bytes 131088 | tf_op jit(solution)/shard_map/jit(_take)/gather | solution.py:120
  96.5 1.8 %gather_fusion.2 = f32[4,8,512]{2,1,0:T(8,128)S(1)} fusion(f32[8,64,512]{2,0,1:T(8,128)} %bitcast.101, s32[1024]{0:T(1024)S(1)} %pad_clamp_fusion.4), kind=kCustom, calls=%fused_computation.2.clone | custom fusion | bytes 131088 | tf_op jit(solution)/shard_map/jit(_take)/gather | solution.py:120
  98.4 66.5 %reduce-scatter.2.cloned.1.call-done = f32[8,2048]{1,0:T(8,128)} async-done(((f32[8,16384]{1,0:T(8,128)}), f32[8,2048]{1,0:T(8,128)}) %reduce-scatter.2.cloned.1.call-update) | async-done | bytes 65552 | tf_op jit(solution)/shard_map/reduce_scatter | solution.py:109
  165.0 0.9 fusion.40
  165.9 0.7 reshape.111
  (36 shorter events, 3.3 us)
Async XLA Ops:
  7.2 81.6 %copy-start = (s32[64,3]{0,1:T(4,128)S(1)}, s32[64,3]{0,1:T(4,128)}, u32[]{:S(2)}) copy-start(s32[64,3]{0,1:T(4,128)} %param.25) | copy-start | bytes 2308
  7.2 74.0 %all-reduce.2.cloned.1.call-start = ((), (), s32[]{:S(2)}) async-start(), calls=%async_computation.1 | async-start | bytes 262144 | tf_op jit(solution)/shard_map/psum | solution.py:102
  35.7 6.8 %copy-start.5 = (f32[4]{0:T(128)S(1)}, f32[4]{0:T(128)}, u32[]{:S(2)}) copy-start(f32[4]{0:T(128)} %param.22) | copy-start | bytes 52
  35.7 7.5 %copy-start.6 = (f32[8,4]{0,1:T(4,128)S(1)}, f32[8,4]{0,1:T(4,128)}, u32[]{:S(2)}) copy-start(f32[8,4]{0,1:T(4,128)} %param.23) | copy-start | bytes 388
  35.7 7.5 %copy-start.4 = (s32[4096]{0:T(1024)S(1)}, s32[4096]{0:T(1024)}, u32[]{:S(2)}) copy-start(s32[4096]{0:T(1024)} %param.21) | copy-start | bytes 49156
  40.9 0.9 copy-start.1
  41.7 51.2 %all-gather.2.cloned.1.call-start = ((), (), s32[]{:S(2)}) async-start(), calls=%async_computation.3 | async-start | bytes 1572864 | tf_op jit(solution)/shard_map/all_gather | solution.py:89
  42.5 122.5 %reduce-scatter.2.cloned.1.call-start = ((), (), s32[]{:S(2)}) async-start(), calls=%async_computation.2 | async-start | bytes 589824 | tf_op jit(solution)/shard_map/reduce_scatter | solution.py:109
  87.6 77.3 %copy-start.3 = (f32[8,1,2048]{2,1,0:T(1,128)S(1)}, f32[8,1,2048]{2,1,0:T(1,128)}, u32[]{:S(2)}) copy-start(f32[8,1,2048]{2,1,0:T(1,128)} %param.16) | copy-start | bytes 196612
  87.7 77.3 %copy-start.7 = (f32[8]{0:T(128)S(1)}, f32[8]{0:T(128)}, u32[]{:S(2)}) copy-start(f32[8]{0:T(128)} %param.24) | copy-start | bytes 100
  87.7 78.9 %copy-start.2 = (f32[8,32,128]{2,0,1:T(8,128)S(1)}, f32[8,32,128]{2,0,1:T(8,128)}, u32[]{:S(2)}) copy-start(f32[8,32,128]{2,0,1:T(8,128)} %all-reduce.2.cloned.1.call-done) | copy-start | bytes 393220
Sparse Core Ops, SparseCore 0:
  41.9 39.2 all-reduce.1
  82.7 10.1 all-gather.1
  96.3 68.5 reduce-scatter.1
where the time goes:
time: 173 us; the launch traced here: 174 us
  waiting for transfers between devices  107 us (62%)
  blocking collectives  27 us (16%)
  between operations  14.6 us (8%)
  local copies, waits for them, and re-layouts  12.8 us (7%)
  other arithmetic  7.33 us (4%)
  matrix products  5.07 us (3%)
    reduce_scatter x1, waiting for transfers between devices, local(): lax.psum_scatter(term.reshape(weight_count, group_width), 'vox', scatter_...  66.5 us
    psum x1, waiting for transfers between devices, local(): dose_blocks = lax.psum(partial_value, 'beam')  35.4 us
    all_gather x1, blocking collectives, local(): own_group = lax.all_gather(fluence, 'vox', axis=2, tiled=True)  27 us
    gather x3, local copies, waits for them, and re-layouts, local(): jnp.take(beam_view, neighbour_rows[:, neighbour], axis=1)  5.32 us
    all_gather x1, waiting for transfers between devices, local(): everything = lax.all_gather(own_group, 'beam', axis=1, tiled=True)  4.1 us
  transfers between devices with their start and end apart: 3, of which 3 were waited for; matrix products, arithmetic and copies ran while one was open for 9% of the time, Pallas kernels for 0%

commit v1 on v0

v1 whole, which is shorter than its diff:
```python
import functools

import jax
import jax.numpy as jnp
from jax import lax
from jax.experimental import pallas as pl
from jax.experimental.pallas import tpu as pltpu
from jax.sharding import PartitionSpec as P

TILE = 128
BLB = 512
MESH = pl.DeviceIdType.MESH
F32 = jnp.float32
BF16 = jnp.bfloat16


def two_terms(x):
    high = x.astype(BF16)
    return high, (x - high.astype(F32)).astype(BF16)


def three_terms(x):
    high = x.astype(BF16)
    rest = x - high.astype(F32)
    middle = rest.astype(BF16)
    return high, middle, (rest - middle.astype(F32)).astype(BF16)


def dot(a, b, on=0):
    return lax.dot_general(a, b, (((1,), (on,)), ((), ())), preferred_element_type=F32)


def kernel(
    parts,
    groups,
    fluence,
    values,
    row_list,
    column_list,
    row_vector,
    column_vector,
    count,
    labels,
    prescribed,
    weights,
    smoothing,
    neighbours,
    dose_out,
    gradient_out,
    tiles,
    split,
    own,
    other,
    product,
    partial,
    partner_partial,
    residual,
    terms,
    arrived,
    base,
    load_sem,
    gather_send,
    gather_recv,
    pair_send,
    pair_recv,
    scatter_send,
    scatter_recv,
):
    me = lax.axis_index("vox")
    group = lax.axis_index("beam")
    partner = lax.rem(group + 1, groups)
    k_count = fluence.shape[0]
    blocks_here = fluence.shape[2] // TILE
    row_blocks = labels.shape[0]
    slots = tiles.shape[0]
    column_blocks = own.shape[0]
    chunks = load_sem.shape[0]
    chunk = slots // chunks
    peers = [lax.rem(me + step, parts) for step in range(1, parts)]

    loads = []
    for part in range(chunks):
        here = pl.ds(part * chunk, chunk)
        copy = pltpu.make_async_copy(values.at[0, 0, here], tiles.at[here], load_sem.at[part])
        copy.start()
        loads.append(copy)

    barrier = pltpu.get_barrier_semaphore()
    for peer in peers:
        pl.semaphore_signal(barrier, inc=1, device_id={"vox": peer}, device_id_type=MESH)
    pl.semaphore_signal(barrier, inc=1, device_id={"beam": partner}, device_id_type=MESH)

    for block in range(blocks_here):
        own[me * blocks_here + block] = fluence[:, 0, block * TILE : (block + 1) * TILE]

    pl.semaphore_wait(barrier, parts)

    mine = pl.ds(me * blocks_here, blocks_here)
    gathers = []
    for step, peer in enumerate(peers):
        copy = pltpu.make_async_remote_copy(
            src_ref=own.at[mine],
            dst_ref=own.at[mine],
            send_sem=gather_send.at[step],
            recv_sem=gather_recv.at[step],
            device_id={"vox": peer},
            device_id_type=MESH,
        )
        copy.start()
        gathers.append(copy)

    for part in range(chunks):
        loads[part].wait()
        for slot in range(part * chunk, (part + 1) * chunk):
            high, low = two_terms(tiles[slot])
            split[slot, :TILE] = high
            split[slot, TILE:] = low

    for copy in gathers:
        copy.wait_recv()

    share = pltpu.make_async_remote_copy(
        src_ref=own,
        dst_ref=other,
        send_sem=pair_send.at[0],
        recv_sem=pair_recv.at[0],
        device_id={"beam": partner},
        device_id_type=MESH,
    )
    share.start()

    for slot in range(slots):
        high, low = two_terms(own[column_list[0, 0, slot]])
        out = dot(jnp.concatenate([high, low], axis=0), split[slot], on=1)
        out = out[:k_count] + out[k_count:]
        product[pl.ds(slot, k_count, stride=slots), :] = out[:, :TILE] + out[:, TILE:]

    active = lax.broadcasted_iota(jnp.int32, (1, slots), 1) < count[0, 0]

    def placed(vector, length):
        blocks = lax.broadcasted_iota(jnp.int32, (length, slots), 0)
        place = jnp.where((vector == blocks) & active, 1.0, 0.0).astype(BF16)
        wide = jnp.concatenate(
            [product[k * slots : (k + 1) * slots, :] for k in range(k_count)], axis=1
        )
        high, middle, low = three_terms(wide)
        return dot(place, high) + (dot(place, middle) + dot(place, low))

    dose = placed(row_vector[0], row_blocks)
    for k in range(k_count):
        partial[k * row_blocks : (k + 1) * row_blocks, :] = dose[:, k * TILE : (k + 1) * TILE]
    swap = pltpu.make_async_remote_copy(
        src_ref=partial,
        dst_ref=partner_partial,
        send_sem=pair_send.at[1],
        recv_sem=pair_recv.at[1],
        device_id={"beam": partner},
        device_id_type=MESH,
    )
    swap.start()

    k_index = lax.broadcasted_iota(jnp.int32, (k_count, TILE), 0)

    def spread_over_k(read):
        column = jnp.zeros((k_count, TILE), F32)
        for k in range(k_count):
            column = jnp.where(k_index == k, read(k), column)
        return column

    weight_of = [
        spread_over_k(lambda k, s=s: weights[k, s]) for s in range(prescribed.shape[0])
    ]
    smooth = spread_over_k(lambda k: smoothing[k])

    swap.wait_recv()
    for row in range(row_blocks):
        where = pl.ds(row, k_count, stride=row_blocks)
        total = partial[where, :] + partner_partial[where, :]
        dose_out[:, row * TILE : (row + 1) * TILE] = total
        label = jnp.broadcast_to(labels[row : row + 1, :], (k_count, TILE))
        target = jnp.zeros((k_count, TILE), F32)
        scaled = jnp.zeros((k_count, TILE), F32)
        for structure in range(prescribed.shape[0]):
            member = label == structure
            target = jnp.where(member, prescribed[structure], target)
            scaled = jnp.where(member, weight_of[structure], scaled)
        excess = total - target
        excess = jnp.where(label == 0, excess, jnp.maximum(excess, 0.0))
        residual[row] = scaled * excess

    for slot in range(slots):
        high, low = two_terms(residual[row_list[0, 0, slot]])
        both = jnp.concatenate([high, low], axis=0)
        out = dot(jnp.concatenate([both, both], axis=1), split[slot])
        product[pl.ds(slot, k_count, stride=slots), :] = out[:k_count] + out[k_count:]

    adjoint = placed(column_vector[0], column_blocks)
    for part in range(parts):
        terms[part] = adjoint[part * blocks_here : (part + 1) * blocks_here, :]
    scatters = []
    for step, peer in enumerate(peers):
        copy = pltpu.make_async_remote_copy(
            src_ref=terms.at[peer],
            dst_ref=arrived.at[step],
            send_sem=scatter_send.at[step],
            recv_sem=scatter_recv.at[step],
            device_id={"vox": peer},
            device_id_type=MESH,
        )
        copy.start()
        scatters.append(copy)

    share.wait_recv()
    per_beam = BLB // TILE
    group_beams = column_blocks // per_beam
    near = neighbours.shape[1]
    for block in range(blocks_here):
        place = group * column_blocks + me * blocks_here + block
        beam = place // per_beam
        within = place % per_beam
        around = jnp.zeros((k_count, TILE), F32)
        for n in range(near):
            beside = neighbours[beam, n]
            in_other = jnp.where(beside >= group_beams, 1, 0)
            at = (beside - in_other * group_beams) * per_beam + within
            around = around + jnp.where(in_other == group, own[at], other[at])
        here = fluence[:, 0, block * TILE : (block + 1) * TILE]
        base[block] = smooth * (near * here - around)

    swap.wait_send()
    total = terms[me]
    for step in range(parts - 1):
        scatters[step].wait_recv()
        total = total + arrived[step]
    for k in range(k_count):
        product_rows = pl.ds(k * blocks_here, blocks_here)
        partial[product_rows, :] = total[:, k * TILE : (k + 1) * TILE]
    for block in range(blocks_here):
        summed = partial[pl.ds(block, k_count, stride=blocks_here), :]
        gradient_out[:, 0, block * TILE : (block + 1) * TILE] = summed + base[block]

    for copy in gathers + scatters:
        copy.wait_send()
    share.wait_send()


def local(
    fluence,
    tile_values,
    tile_rows,
    tile_columns,
    tile_count,
    labels,
    prescribed,
    weights,
    smoothing,
    beam_neighbours,
):
    groups = lax.axis_size("beam")
    parts = lax.axis_size("vox")
    k_count, _, shard = fluence.shape
    blocks_here = shard // TILE
    column_blocks = blocks_here * parts
    row_blocks = labels.shape[0] // TILE
    slots = tile_values.shape[2]
    chunks = 4
    vmem = pl.BlockSpec(memory_space=pltpu.VMEM)
    smem = pl.BlockSpec(memory_space=pltpu.SMEM)
    dma = pltpu.SemaphoreType.DMA
    return pl.pallas_call(
        functools.partial(kernel, parts, groups),
        out_shape=(
            jax.ShapeDtypeStruct((k_count, row_blocks * TILE), F32),
            jax.ShapeDtypeStruct(fluence.shape, F32),
        ),
        in_specs=[
            vmem,
            pl.BlockSpec(memory_space=pl.ANY),
            smem,
            smem,
            vmem,
            vmem,
            smem,
            vmem,
            smem,
            smem,
            smem,
            smem,
        ],
        out_specs=(vmem, vmem),
        scratch_shapes=[
            pltpu.VMEM((slots, TILE, TILE), F32),
            pltpu.VMEM((slots, 2 * TILE, TILE), BF16),
            pltpu.VMEM((column_blocks, k_count, TILE), F32),
            pltpu.VMEM((column_blocks, k_count, TILE), F32),
            pltpu.VMEM((k_count * slots, TILE), F32),
            pltpu.VMEM((k_count * row_blocks, TILE), F32),
            pltpu.VMEM((k_count * row_blocks, TILE), F32),
            pltpu.VMEM((row_blocks, k_count, TILE), F32),
            pltpu.VMEM((parts, blocks_here, k_count * TILE), F32),
            pltpu.VMEM((parts - 1, blocks_here, k_count * TILE), F32),
            pltpu.VMEM((blocks_here, k_count, TILE), F32),
            dma((chunks,)),
            dma((parts - 1,)),
            dma((parts - 1,)),
            dma((2,)),
            dma((2,)),
            dma((parts - 1,)),
            dma((parts - 1,)),
        ],
        compiler_params=pltpu.CompilerParams(
            collective_id=0, has_side_effects=True, vmem_limit_bytes=40 * 1024 * 1024
        ),
    )(
        fluence,
        tile_values,
        tile_rows,
        tile_columns,
        tile_rows,
        tile_columns,
        tile_count,
        labels.reshape(row_blocks, TILE),
        prescribed,
        weights,
        smoothing,
        beam_neighbours,
    )


def solution(mesh):
    return jax.shard_map(
        local,
        mesh=mesh,
        in_specs=(
            P("plans", "beam", "vox"),
            P(("plans", "vox"), "beam", None, None, None),
            P(("plans", "vox"), "beam", None),
            P(("plans", "vox"), "beam", None),
            P(("plans", "vox"), "beam"),
            P(("plans", "vox")),
            P("plans"),
            P("plans", None),
            P("plans"),
            P("plans", None),
        ),
        out_specs=(P("plans", "vox"), P("plans", "beam", "vox")),
        check_vma=False,
    )
```

time: 173 us -> 43.4 us (0.25)
  the two profiles are of different devices: /device:TPU:1 before, /device:TPU:31 now
where the time goes in v1:
time: 43.4 us; the launch traced here: 43.1 us
  Pallas kernels  33.2 us (76%)
  local copies, waits for them, and re-layouts  8.58 us (20%)
  between operations  1.29 us (3%)
    pallas_call x1, Pallas kernels, local(): pl.pallas_call(functools.partial(kernel, parts, groups), out_shape=(jax.S...  33.2 us
    unnamed x18, local copies, waits for them, and re-layouts  8.58 us

profile of v1, /device:TPU:31, one launch (start us, length us, event | category | flops | bytes accessed | tf_op | source)
XLA Modules:
  0.0 43.1 jit_solution(17491790661641181630)
XLA Ops:
  1.3 0.8 %copy.12.weights = f32[8,4]{1,0:T(8,128)S(1)} copy(f32[8,4]{0,1:T(4,128)} %param.17) | data formatting | bytes 256 | tf_op args[7]
  2.0 0.8 %copy.13.neighbours = s32[64,3]{1,0:T(8,128)S(1)} copy(s32[64,3]{0,1:T(4,128)} %param.19) | data formatting | bytes 1536 | tf_op args[9]
  2.8 0.0 copy-start
  2.8 1.6 %copy-done = f32[1,1,32,128,128]{4,3,2,1,0:T(8,128)S(1)} copy-done((f32[1,1,32,128,128]{4,3,2,1,0:T(8,128)S(1)}, f32[1,1,32,128,128]{4,3,2,1,0:T(8,128)}, u32[]{:S(2)}) %copy-start) | copy-done | bytes 2097176
  4.4 0.0 copy-start.1
  4.4 0.8 %copy-done.1 = f32[8,1,2048]{2,1,0:T(1,128)S(1)} copy-done((f32[8,1,2048]{2,1,0:T(1,128)S(1)}, f32[8,1,2048]{2,1,0:T(1,128)}, u32[]{:S(2)}) %copy-start.1) | copy-done | bytes 65560
  5.2 0.0 copy-start.2
  5.2 0.7 %copy-done.2 = s32[4096]{0:T(1024)S(1)} copy-done((s32[4096]{0:T(1024)S(1)}, s32[4096]{0:T(1024)}, u32[]{:S(2)}) %copy-start.2) | copy-done | bytes 16408
  6.0 0.0 copy-start.3
  6.0 0.7 %copy-done.3 = s32[1,1,32]{2,1,0:T(1,128)S(1)} copy-done((s32[1,1,32]{2,1,0:T(1,128)S(1)}, s32[1,1,32]{2,1,0:T(1,128)}, u32[]{:S(2)}) %copy-start.3) | copy-done | bytes 152
  6.6 0.0 copy-start.4
  6.6 0.7 %copy-done.4 = s32[1,1,32]{2,1,0:T(1,128)S(1)} copy-done((s32[1,1,32]{2,1,0:T(1,128)S(1)}, s32[1,1,32]{2,1,0:T(1,128)}, u32[]{:S(2)}) %copy-start.4) | copy-done | bytes 152
  7.3 0.0 copy-start.5
  7.3 0.7 %copy-done.5 = f32[4]{0:T(128)S(1)} copy-done((f32[4]{0:T(128)S(1)}, f32[4]{0:T(128)}, u32[]{:S(2)}) %copy-start.5) | copy-done | bytes 40
  7.9 0.0 copy-start.6
  7.9 0.7 %copy-done.6 = f32[8]{0:T(128)S(1)} copy-done((f32[8]{0:T(128)S(1)}, f32[8]{0:T(128)}, u32[]{:S(2)}) %copy-start.6) | copy-done | bytes 56
  8.6 33.2 %shard_map.113 = (f32[8,4096]{1,0:T(8,128)S(1)}, f32[8,1,2048]{2,1,0:T(1,128)S(1)}) custom-call(f32[8,1,2048]{2,1,0:T(1,128)S(1)} %copy-done.1, f32[1,1,32,128,128]{4,3,2,1,0:T(8,128)S(1)} %copy-done, s32[1,1,32]{2,1,0:T(1,128)S(1)} %copy-done.3, s32[1,1,32]{2,1,0:T(1,128)S(1)} %copy-done.4, s32[1,1,32]{2,1,0:T(1,128)S(1)} %copy-done.3, ...), custom_call_target="tpu_custom_call" | custom-call | tf_op jit(solution)/shard_map/pallas_call | solution.py:270
  41.8 0.7 %copy.17 = f32[8,4096]{1,0:T(8,128)} copy(f32[8,4096]{1,0:T(8,128)S(1)} %get-tuple-element.4) | data formatting | bytes 262144
  42.4 0.6 %copy.18 = f32[8,1,2048]{2,1,0:T(1,128)} copy(f32[8,1,2048]{2,1,0:T(1,128)S(1)} %get-tuple-element.5) | data formatting | bytes 131072
Async XLA Ops:
  2.8 1.6 %copy-start = (f32[1,1,32,128,128]{4,3,2,1,0:T(8,128)S(1)}, f32[1,1,32,128,128]{4,3,2,1,0:T(8,128)}, u32[]{:S(2)}) copy-start(f32[1,1,32,128,128]{4,3,2,1,0:T(8,128)} %values.1) | copy-start | bytes 6291460
  4.4 0.8 %copy-start.1 = (f32[8,1,2048]{2,1,0:T(1,128)S(1)}, f32[8,1,2048]{2,1,0:T(1,128)}, u32[]{:S(2)}) copy-start(f32[8,1,2048]{2,1,0:T(1,128)} %fluence.1) | copy-start | bytes 196612
  5.2 0.7 %copy-start.2 = (s32[4096]{0:T(1024)S(1)}, s32[4096]{0:T(1024)}, u32[]{:S(2)}) copy-start(s32[4096]{0:T(1024)} %param.15) | copy-start | bytes 49156
  6.0 0.7 %copy-start.3 = (s32[1,1,32]{2,1,0:T(1,128)S(1)}, s32[1,1,32]{2,1,0:T(1,128)}, u32[]{:S(2)}) copy-start(s32[1,1,32]{2,1,0:T(1,128)} %row_vector.1) | copy-start | bytes 388
  6.6 0.7 %copy-start.4 = (s32[1,1,32]{2,1,0:T(1,128)S(1)}, s32[1,1,32]{2,1,0:T(1,128)}, u32[]{:S(2)}) copy-start(s32[1,1,32]{2,1,0:T(1,128)} %column_vector.1) | copy-start | bytes 388
  7.3 0.7 %copy-start.5 = (f32[4]{0:T(128)S(1)}, f32[4]{0:T(128)}, u32[]{:S(2)}) copy-start(f32[4]{0:T(128)} %prescribed.1) | copy-start | bytes 52
  7.9 0.7 %copy-start.6 = (f32[8]{0:T(128)S(1)}, f32[8]{0:T(128)}, u32[]{:S(2)}) copy-start(f32[8]{0:T(128)} %smoothing.1) | copy-start | bytes 100

commit v2 on v1

v2 whole, which is shorter than its diff:
```python
import functools

import jax
import jax.numpy as jnp
from jax import lax
from jax.experimental import pallas as pl
from jax.experimental.pallas import tpu as pltpu
from jax.sharding import PartitionSpec as P

TILE = 128
BLB = 512
MESH = pl.DeviceIdType.MESH
F32 = jnp.float32
BF16 = jnp.bfloat16


def two_terms(x):
    high = x.astype(BF16)
    return high, (x - high.astype(F32)).astype(BF16)


def three_terms(x):
    high = x.astype(BF16)
    rest = x - high.astype(F32)
    middle = rest.astype(BF16)
    return high, middle, (rest - middle.astype(F32)).astype(BF16)


def dot(a, b, on=0):
    return lax.dot_general(a, b, (((1,), (on,)), ((), ())), preferred_element_type=F32)


def kernel(
    wide_parts,
    tall_parts,
    groups,
    fluence_in,
    values,
    row_in,
    column_in,
    count_in,
    labels_in,
    prescribed_in,
    weights_in,
    smoothing_in,
    neighbours_in,
    dose_out,
    gradient_out,
    fluence,
    row_list,
    column_list,
    row_vector,
    column_vector,
    count,
    labels,
    prescribed,
    weights,
    smoothing,
    neighbours,
    tiles,
    split,
    own,
    other,
    product,
    partial,
    partner_partial,
    target,
    scaled,
    residual,
    terms,
    beside_terms,
    middle_terms,
    far_terms,
    base,
    small_sem,
    load_sem,
    tall_send,
    tall_recv,
    wide_send,
    wide_recv,
    pair_send,
    pair_recv,
    first_send,
    first_recv,
    second_send,
    second_recv,
):
    me = lax.axis_index("vox")
    group = lax.axis_index("beam")
    partner = lax.rem(group + 1, groups)
    tall, wide = me // wide_parts, me % wide_parts
    k_count = fluence.shape[0]
    blocks_here = fluence.shape[2] // TILE
    row_blocks = labels.shape[0]
    slots = tiles.shape[0]
    column_blocks = own.shape[0]
    structures = prescribed.shape[0]
    chunks = load_sem.shape[0]
    chunk = slots // chunks
    tall_at = [lax.rem(tall + step, tall_parts) for step in range(tall_parts)]
    tall_from = [lax.rem(tall + tall_parts - step, tall_parts) for step in range(tall_parts)]
    tall_peers = [at * wide_parts + wide for at in tall_at]
    wide_peers = [
        tall * wide_parts + lax.rem(wide + step, wide_parts) for step in range(wide_parts)
    ]

    def remote(source, target_ref, send, recv, axis, peer):
        copy = pltpu.make_async_remote_copy(
            src_ref=source,
            dst_ref=target_ref,
            send_sem=send,
            recv_sem=recv,
            device_id={axis: peer},
            device_id_type=MESH,
        )
        copy.start()
        return copy

    barrier = pltpu.get_barrier_semaphore()
    for peer in tall_peers[1:] + wide_peers[1:]:
        pl.semaphore_signal(barrier, inc=1, device_id={"vox": peer}, device_id_type=MESH)
    pl.semaphore_signal(barrier, inc=1, device_id={"beam": partner}, device_id_type=MESH)

    small = []
    for index, (source, place) in enumerate(
        (
            (fluence_in, fluence),
            (labels_in, labels),
            (prescribed_in, prescribed),
            (weights_in, weights),
            (column_in, column_list),
            (column_in, column_vector),
            (row_in, row_list),
            (row_in, row_vector),
            (count_in, count),
            (smoothing_in, smoothing),
            (neighbours_in, neighbours),
        )
    ):
        copy = pltpu.make_async_copy(source, place, small_sem.at[index])
        copy.start()
        small.append(copy)
    loads = []
    for part in range(chunks):
        here = pl.ds(part * chunk, chunk)
        copy = pltpu.make_async_copy(values.at[0, 0, here], tiles.at[here], load_sem.at[part])
        copy.start()
        loads.append(copy)

    small[0].wait()
    for block in range(blocks_here):
        own[me * blocks_here + block] = fluence[:, 0, block * TILE : (block + 1) * TILE]

    pl.semaphore_wait(barrier, tall_parts + wide_parts - 1)

    def shard_of(part):
        return own.at[pl.ds(part * blocks_here, blocks_here)]

    def along_wide(step, part):
        return [
            remote(
                shard_of(part),
                shard_of(part),
                wide_send.at[step, near],
                wide_recv.at[step, near],
                "vox",
                wide_peers[near + 1],
            )
            for near in range(wide_parts - 1)
        ]

    tall_copies = [
        remote(
            shard_of(me),
            shard_of(me),
            tall_send.at[step - 1],
            tall_recv.at[step - 1],
            "vox",
            tall_peers[step],
        )
        for step in range(1, tall_parts)
    ]
    wide_copies = along_wide(0, me)

    def split_chunk(part):
        loads[part].wait()
        for slot in range(part * chunk, (part + 1) * chunk):
            high, low = two_terms(tiles[slot])
            split[slot, :TILE] = high
            split[slot, TILE:] = low

    for copy in small[1:]:
        copy.wait()
    k_index = lax.broadcasted_iota(jnp.int32, (k_count, TILE), 0)

    def spread_over_k(read):
        column = jnp.zeros((k_count, TILE), F32)
        for k in range(k_count):
            column = jnp.where(k_index == k, read(k), column)
        return column

    def structure_values():
        weight_of = [spread_over_k(lambda k, s=s: weights[s, k]) for s in range(structures)]
        for row in range(row_blocks):
            label = jnp.broadcast_to(labels[row : row + 1, :], (k_count, TILE))
            level = jnp.zeros((k_count, TILE), F32)
            factor = jnp.zeros((k_count, TILE), F32)
            for structure in range(structures):
                member = label == structure
                level = jnp.where(member, prescribed[structure], level)
                factor = jnp.where(member, weight_of[structure], factor)
            target[row] = level
            scaled[row] = factor

    for part in range(chunks // 2):
        split_chunk(part)
    work = [functools.partial(split_chunk, part) for part in range(chunks // 2, chunks)]
    work.append(structure_values)
    for step in range(1, tall_parts):
        tall_copies[step - 1].wait_recv()
        wide_copies += along_wide(step, tall_from[step] * wide_parts + wide)
        if work:
            work.pop(0)()
    for piece in work:
        piece()
    for copy in wide_copies:
        copy.wait_recv()

    share = remote(own, other, pair_send.at[0], pair_recv.at[0], "beam", partner)

    for slot in range(slots):
        high, low = two_terms(own[column_list[0, 0, slot]])
        out = dot(jnp.concatenate([high, low], axis=0), split[slot], on=1)
        out = out[:k_count] + out[k_count:]
        product[pl.ds(slot, k_count, stride=slots), :] = out[:, :TILE] + out[:, TILE:]

    active = lax.broadcasted_iota(jnp.int32, (1, slots), 1) < count[0, 0]

    def products():
        return three_terms(
            jnp.concatenate(
                [product[k * slots : (k + 1) * slots, :] for k in range(k_count)], axis=1
            )
        )

    def placed(vector, blocks, three):
        place = jnp.where((vector == blocks) & active, 1.0, 0.0).astype(BF16)
        high, middle, low = three
        return dot(place, high) + (dot(place, middle) + dot(place, low))

    dose = placed(
        row_vector[0], lax.broadcasted_iota(jnp.int32, (row_blocks, slots), 0), products()
    )
    for k in range(k_count):
        partial[k * row_blocks : (k + 1) * row_blocks, :] = dose[:, k * TILE : (k + 1) * TILE]
    swap = remote(partial, partner_partial, pair_send.at[1], pair_recv.at[1], "beam", partner)
    swap.wait_recv()
    for row in range(row_blocks):
        where = pl.ds(row, k_count, stride=row_blocks)
        total = partial[where, :] + partner_partial[where, :]
        dose_out[:, row * TILE : (row + 1) * TILE] = total
        label = jnp.broadcast_to(labels[row : row + 1, :], (k_count, TILE))
        excess = total - target[row]
        excess = jnp.where(label == 0, excess, jnp.maximum(excess, 0.0))
        residual[row] = scaled[row] * excess

    for slot in range(slots):
        high, low = two_terms(residual[row_list[0, 0, slot]])
        both = jnp.concatenate([high, low], axis=0)
        out = dot(jnp.concatenate([both, both], axis=1), split[slot])
        product[pl.ds(slot, k_count, stride=slots), :] = out[:k_count] + out[k_count:]

    three = products()
    line = lax.broadcasted_iota(jnp.int32, (tall_parts * blocks_here, slots), 0)
    line_tall, line_block = line // blocks_here, line % blocks_here

    def make_terms(near):
        at = lax.rem(wide + near, wide_parts)
        found = placed(column_vector[0], (line_tall * wide_parts + at) * blocks_here + line_block, three)
        for part in range(tall_parts):
            terms[near, part] = found[part * blocks_here : (part + 1) * blocks_here, :]

    steps = list(range(1, tall_parts)) + [0]
    first_copies = {step: [] for step in steps}
    for near in range(1, wide_parts):
        make_terms(near)
        for step in steps:
            first_copies[step].append(
                remote(
                    terms.at[near, tall_at[step]],
                    beside_terms.at[step, near - 1],
                    first_send.at[step, near - 1],
                    first_recv.at[step, near - 1],
                    "vox",
                    wide_peers[near],
                )
            )
    make_terms(0)

    def gathered(step):
        total = terms[0, tall_at[step]]
        for near, copy in enumerate(first_copies[step]):
            copy.wait_recv()
            total = total + beside_terms[step, near]
        return total

    second_copies = []
    for step in range(1, tall_parts):
        middle_terms[step - 1] = gathered(step)
        second_copies.append(
            remote(
                middle_terms.at[step - 1],
                far_terms.at[step - 1],
                second_send.at[step - 1],
                second_recv.at[step - 1],
                "vox",
                tall_peers[step],
            )
        )

    share.wait_recv()
    smooth = spread_over_k(lambda k: smoothing[k])
    per_beam = BLB // TILE
    group_beams = column_blocks // per_beam
    near_count = neighbours.shape[0]
    for block in range(blocks_here):
        place = group * column_blocks + me * blocks_here + block
        beam = place // per_beam
        within = place % per_beam
        around = jnp.zeros((k_count, TILE), F32)
        for n in range(near_count):
            beside = neighbours[n, beam]
            beside_group = jnp.where(beside >= group_beams, 1, 0)
            at = (beside - beside_group * group_beams) * per_beam + within
            around = around + jnp.where(beside_group == group, own[at], other[at])
        here = fluence[:, 0, block * TILE : (block + 1) * TILE]
        base[block] = smooth * (near_count * here - around)

    swap.wait_send()
    total = gathered(0)
    for copy_index, copy in enumerate(second_copies):
        copy.wait_recv()
        total = total + far_terms[copy_index]
    for k in range(k_count):
        partial[k * blocks_here : (k + 1) * blocks_here, :] = total[:, k * TILE : (k + 1) * TILE]
    for block in range(blocks_here):
        summed = partial[pl.ds(block, k_count, stride=blocks_here), :]
        gradient_out[:, 0, block * TILE : (block + 1) * TILE] = summed + base[block]

    for copy in tall_copies + wide_copies + second_copies + [share]:
        copy.wait_send()
    for copies in first_copies.values():
        for copy in copies:
            copy.wait_send()


def local(
    fluence,
    tile_values,
    tile_rows,
    tile_columns,
    tile_count,
    labels,
    prescribed,
    weights,
    smoothing,
    beam_neighbours,
):
    groups = lax.axis_size("beam")
    parts = lax.axis_size("vox")
    wide_parts = max(w for w in range(1, parts + 1) if parts % w == 0 and w * w <= parts)
    tall_parts = parts // wide_parts
    k_count, _, shard = fluence.shape
    blocks_here = shard // TILE
    column_blocks = blocks_here * parts
    row_blocks = labels.shape[0] // TILE
    slots = tile_values.shape[2]
    chunks = 4
    width = k_count * TILE
    operands = (
        fluence,
        tile_values,
        tile_rows,
        tile_columns,
        tile_count,
        labels.reshape(row_blocks, TILE),
        prescribed,
        weights.T,
        smoothing,
        beam_neighbours.T,
    )

    def on_chip(array, space):
        return space(array.shape, array.dtype)

    vmem, smem = pltpu.VMEM, pltpu.SMEM
    dma = pltpu.SemaphoreType.DMA
    out = pl.BlockSpec(memory_space=pltpu.VMEM)
    return pl.pallas_call(
        functools.partial(kernel, wide_parts, tall_parts, groups),
        out_shape=(
            jax.ShapeDtypeStruct((k_count, row_blocks * TILE), F32),
            jax.ShapeDtypeStruct(fluence.shape, F32),
        ),
        in_specs=[pl.BlockSpec(memory_space=pltpu.HBM)] * len(operands),
        out_specs=(out, out),
        scratch_shapes=[
            on_chip(fluence, vmem),
            on_chip(tile_rows, smem),
            on_chip(tile_columns, smem),
            on_chip(tile_rows, vmem),
            on_chip(tile_columns, vmem),
            on_chip(tile_count, smem),
            on_chip(operands[5], vmem),
            on_chip(prescribed, smem),
            on_chip(operands[7], smem),
            on_chip(smoothing, smem),
            on_chip(operands[9], smem),
            vmem((slots, TILE, TILE), F32),
            vmem((slots, 2 * TILE, TILE), BF16),
            vmem((column_blocks, k_count, TILE), F32),
            vmem((column_blocks, k_count, TILE), F32),
            vmem((k_count * slots, TILE), F32),
            vmem((k_count * row_blocks, TILE), F32),
            vmem((k_count * row_blocks, TILE), F32),
            vmem((row_blocks, k_count, TILE), F32),
            vmem((row_blocks, k_count, TILE), F32),
            vmem((row_blocks, k_count, TILE), F32),
            vmem((wide_parts, tall_parts, blocks_here, width), F32),
            vmem((tall_parts, wide_parts - 1, blocks_here, width), F32),
            vmem((tall_parts - 1, blocks_here, width), F32),
            vmem((tall_parts - 1, blocks_here, width), F32),
            vmem((blocks_here, k_count, TILE), F32),
            dma((11,)),
            dma((chunks,)),
            dma((tall_parts - 1,)),
            dma((tall_parts - 1,)),
            dma((tall_parts, wide_parts - 1)),
            dma((tall_parts, wide_parts - 1)),
            dma((2,)),
            dma((2,)),
            dma((tall_parts, wide_parts - 1)),
            dma((tall_parts, wide_parts - 1)),
            dma((tall_parts - 1,)),
            dma((tall_parts - 1,)),
        ],
        compiler_params=pltpu.CompilerParams(
            collective_id=0, has_side_effects=True, vmem_limit_bytes=58 * 1024 * 1024
        ),
    )(*operands)


def solution(mesh):
    return jax.shard_map(
        local,
        mesh=mesh,
        in_specs=(
            P("plans", "beam", "vox"),
            P(("plans", "vox"), "beam", None, None, None),
            P(("plans", "vox"), "beam", None),
            P(("plans", "vox"), "beam", None),
            P(("plans", "vox"), "beam"),
            P(("plans", "vox")),
            P("plans"),
            P("plans", None),
            P("plans"),
            P("plans", None),
        ),
        out_specs=(P("plans", "vox"), P("plans", "beam", "vox")),
        check_vma=False,
    )
```

time: 43.4 us -> 33.8 us (0.78)
  the two profiles are of different devices: /device:TPU:31 before, /device:TPU:1 now
where the time goes in v2:
time: 33.8 us; the launch traced here: 33.5 us
  Pallas kernels  29.2 us (86%)
  local copies, waits for them, and re-layouts  3.04 us (9%)
  between operations  1.29 us (4%)
    pallas_call x1, Pallas kernels, local(): pl.pallas_call(functools.partial(kernel, wide_parts, tall_parts, groups),...  29.2 us
    unnamed x2, local copies, waits for them, and re-layouts  3.04 us

profile of v2, /device:TPU:1, one launch (start us, length us, event | category | flops | bytes accessed | tf_op | source)
XLA Modules:
  0.0 33.5 jit_solution(2760001909581345460)
XLA Ops:
  1.3 29.2 %shard_map.113 = (f32[8,4096]{1,0:T(8,128)}, f32[8,1,2048]{2,1,0:T(1,128)}) custom-call(f32[8,1,2048]{2,1,0:T(1,128)} %fluence_in.1, f32[1,1,32,128,128]{4,3,2,1,0:T(8,128)} %values.1, s32[1,1,32]{2,1,0:T(1,128)} %row_in.1, s32[1,1,32]{2,1,0:T(1,128)} %column_in.1, s32[1,1]{1,0:T(1,128)S(6)} %copy.14.count_in, s32[32,128]{1,0:T(8,128)} %bitcast.3, ...), custom_call_target="tpu_custom_call" | custom-call | tf_op jit(solution)/shard_map/pallas_call | solution.py:399
  30.5 1.6 %copy.15 = f32[8,4096]{1,0:T(8,128)} copy(f32[8,4096]{1,0:T(8,128)} %get-tuple-element.4) | data formatting | bytes 262144
  32.1 1.5 %copy.16 = f32[8,1,2048]{2,1,0:T(1,128)} copy(f32[8,1,2048]{2,1,0:T(1,128)} %get-tuple-element.5) | data formatting | bytes 131072

commit v3 on v2

--- a/solution.py
+++ b/solution.py
@@ -445,9 +445,9 @@
             dma((tall_parts - 1,)),
         ],
         compiler_params=pltpu.CompilerParams(
-            collective_id=0, has_side_effects=True, vmem_limit_bytes=58 * 1024 * 1024
+            collective_id=0, has_side_effects=True, vmem_limit_bytes=40 * 1024 * 1024
         ),
-    )(*operands)
+    )(*[x if x is tile_count else pltpu.with_memory_space_constraint(x, pltpu.HBM) for x in operands])
 
 
 def solution(mesh):

time: 33.8 us -> 31.3 us (0.926)
  local copies, waits for them, and re-layouts: 3.04 us -> 1.29 us
  Pallas kernels: 29.2 us -> 28.5 us
    unnamed x2, local copies, waits for them, and re-layouts: 3.04 us -> 1.29 us
    pallas_call x1, Pallas kernels: 29.2 us -> 28.5 us  [local(): pl.pallas_call(functools.partial(kernel, wide_parts, tall_parts, groups),...]
where the time goes in v3:
time: 31.3 us; the launch traced here: 31.1 us
  Pallas kernels  28.5 us (91%)
  local copies, waits for them, and re-layouts  1.29 us (4%)
  between operations  1.29 us (4%)
    pallas_call x1, Pallas kernels, local(): pl.pallas_call(functools.partial(kernel, wide_parts, tall_parts, groups),...  28.5 us
    unnamed x2, local copies, waits for them, and re-layouts  1.29 us

profile of v3, /device:TPU:1, one launch (start us, length us, event | category | flops | bytes accessed | tf_op | source)
XLA Modules:
  0.0 31.1 jit_solution(626737684827387543)
XLA Ops:
  1.3 28.5 %shard_map.113 = (f32[8,4096]{1,0:T(8,128)S(1)}, f32[8,1,2048]{2,1,0:T(1,128)S(1)}) custom-call(f32[8,1,2048]{2,1,0:T(1,128)} %fluence_in.1, f32[1,1,32,128,128]{4,3,2,1,0:T(8,128)} %values.1, s32[1,1,32]{2,1,0:T(1,128)} %row_in.1, s32[1,1,32]{2,1,0:T(1,128)} %column_in.1, s32[1,1]{1,0:T(1,128)S(6)} %copy.14.count_in, s32[32,128]{1,0:T(8,128)} %bitcast.3, ...), custom_call_target="tpu_custom_call" | custom-call | tf_op jit(solution)/shard_map/pallas_call | solution.py:399
  29.8 0.7 %copy.15 = f32[8,4096]{1,0:T(8,128)} copy(f32[8,4096]{1,0:T(8,128)S(1)} %get-tuple-element.4) | data formatting | bytes 262144
  30.5 0.6 %copy.16 = f32[8,1,2048]{2,1,0:T(1,128)} copy(f32[8,1,2048]{2,1,0:T(1,128)S(1)} %get-tuple-element.5) | data formatting | bytes 131072

commit v4 on v3

--- a/solution.py
+++ b/solution.py
@@ -153,34 +153,38 @@
 
     pl.semaphore_wait(barrier, tall_parts + wide_parts - 1)
 
-    def shard_of(part):
-        return own.at[pl.ds(part * blocks_here, blocks_here)]
-
-    def along_wide(step, part):
+    pieces = tall_send.shape[1]
+    piece_blocks = blocks_here // pieces
+
+    def shard_of(part, piece):
+        return own.at[pl.ds(part * blocks_here + piece * piece_blocks, piece_blocks)]
+
+    def along_wide(step, part, piece):
         return [
             remote(
-                shard_of(part),
-                shard_of(part),
-                wide_send.at[step, near],
-                wide_recv.at[step, near],
+                shard_of(part, piece),
+                shard_of(part, piece),
+                wide_send.at[step, near, piece],
+                wide_recv.at[step, near, piece],
                 "vox",
                 wide_peers[near + 1],
             )
             for near in range(wide_parts - 1)
         ]
 
-    tall_copies = [
-        remote(
-            shard_of(me),
-            shard_of(me),
-            tall_send.at[step - 1],
-            tall_recv.at[step - 1],
-            "vox",
-            tall_peers[step],
-        )
-        for step in range(1, tall_parts)
-    ]
-    wide_copies = along_wide(0, me)
+    wide_copies = []
+    tall_copies = {}
+    for piece in range(pieces):
+        wide_copies += along_wide(0, me, piece)
+        for step in range(1, tall_parts):
+            tall_copies[step, piece] = remote(
+                shard_of(me, piece),
+                shard_of(me, piece),
+                tall_send.at[step - 1, piece],
+                tall_recv.at[step - 1, piece],
+                "vox",
+                tall_peers[step],
+            )
 
     def split_chunk(part):
         loads[part].wait()
@@ -216,11 +220,12 @@
         split_chunk(part)
     work = [functools.partial(split_chunk, part) for part in range(chunks // 2, chunks)]
     work.append(structure_values)
-    for step in range(1, tall_parts):
-        tall_copies[step - 1].wait_recv()
-        wide_copies += along_wide(step, tall_from[step] * wide_parts + wide)
-        if work:
-            work.pop(0)()
+    for piece in range(pieces):
+        for step in range(1, tall_parts):
+            tall_copies[step, piece].wait_recv()
+            wide_copies += along_wide(step, tall_from[step] * wide_parts + wide, piece)
+            if work:
+                work.pop(0)()
     for piece in work:
         piece()
     for copy in wide_copies:
@@ -347,7 +352,7 @@
         summed = partial[pl.ds(block, k_count, stride=blocks_here), :]
         gradient_out[:, 0, block * TILE : (block + 1) * TILE] = summed + base[block]
 
-    for copy in tall_copies + wide_copies + second_copies + [share]:
+    for copy in list(tall_copies.values()) + wide_copies + second_copies + [share]:
         copy.wait_send()
     for copies in first_copies.values():
         for copy in copies:
@@ -376,6 +381,7 @@
     row_blocks = labels.shape[0] // TILE
     slots = tile_values.shape[2]
     chunks = 4
+    pieces = 2 if blocks_here % 2 == 0 else 1
     width = k_count * TILE
     operands = (
         fluence,
@@ -433,10 +439,10 @@
             vmem((blocks_here, k_count, TILE), F32),
             dma((11,)),
             dma((chunks,)),
-            dma((tall_parts - 1,)),
-            dma((tall_parts - 1,)),
-            dma((tall_parts, wide_parts - 1)),
-            dma((tall_parts, wide_parts - 1)),
+            dma((tall_parts - 1, pieces)),
+            dma((tall_parts - 1, pieces)),
+            dma((tall_parts, wide_parts - 1, pieces)),
+            dma((tall_parts, wide_parts - 1, pieces)),
             dma((2,)),
             dma((2,)),
             dma((tall_parts, wide_parts - 1)),

time: 31.3 us -> 31.4 us (level)
  no operation moved by 1% of the time
where the time goes in v4:
time: 31.4 us; the launch traced here: 30.9 us
  Pallas kernels  28.3 us (90%)
  local copies, waits for them, and re-layouts  1.29 us (4%)
  between operations  1.29 us (4%)
    pallas_call x1, Pallas kernels, local(): pl.pallas_call(functools.partial(kernel, wide_parts, tall_parts, groups),...  28.3 us
    unnamed x2, local copies, waits for them, and re-layouts  1.29 us

profile of v4, /device:TPU:1, one launch (start us, length us, event | category | flops | bytes accessed | tf_op | source)
XLA Modules:
  0.0 30.9 jit_solution(10529747641658939472)
XLA Ops:
  1.3 28.3 %shard_map.113 = (f32[8,4096]{1,0:T(8,128)S(1)}, f32[8,1,2048]{2,1,0:T(1,128)S(1)}) custom-call(f32[8,1,2048]{2,1,0:T(1,128)} %fluence_in.1, f32[1,1,32,128,128]{4,3,2,1,0:T(8,128)} %values.1, s32[1,1,32]{2,1,0:T(1,128)} %row_in.1, s32[1,1,32]{2,1,0:T(1,128)} %column_in.1, s32[1,1]{1,0:T(1,128)S(6)} %copy.14.count_in, s32[32,128]{1,0:T(8,128)} %bitcast.3, ...), custom_call_target="tpu_custom_call" | custom-call | tf_op jit(solution)/shard_map/pallas_call | solution.py:405
  29.6 0.7 %copy.15 = f32[8,4096]{1,0:T(8,128)} copy(f32[8,4096]{1,0:T(8,128)S(1)} %get-tuple-element.4) | data formatting | bytes 262144
  30.3 0.6 %copy.16 = f32[8,1,2048]{2,1,0:T(1,128)} copy(f32[8,1,2048]{2,1,0:T(1,128)S(1)} %get-tuple-element.5) | data formatting | bytes 131072

commit v5 on v3

--- a/solution.py
+++ b/solution.py
@@ -281,42 +281,45 @@
             terms[near, part] = found[part * blocks_here : (part + 1) * blocks_here, :]
 
     steps = list(range(1, tall_parts)) + [0]
-    first_copies = {step: [] for step in steps}
+    halves = [pl.ds(half * (k_count // 2) * TILE, k_count // 2 * TILE) for half in range(2)]
+    first_copies = {(step, half): [] for step in steps for half in range(2)}
     for near in range(1, wide_parts):
         make_terms(near)
-        for step in steps:
-            first_copies[step].append(
+        for half, lanes in enumerate(halves):
+            for step in steps:
+                first_copies[step, half].append(
+                    remote(
+                        terms.at[near, tall_at[step], :, lanes],
+                        beside_terms.at[step, near - 1, :, lanes],
+                        first_send.at[step, near - 1, half],
+                        first_recv.at[step, near - 1, half],
+                        "vox",
+                        wide_peers[near],
+                    )
+                )
+    make_terms(0)
+
+    def gathered(step, half):
+        total = terms[0, tall_at[step], :, halves[half]]
+        for near, copy in enumerate(first_copies[step, half]):
+            copy.wait_recv()
+            total = total + beside_terms[step, near, :, halves[half]]
+        return total
+
+    second_copies = []
+    for half, lanes in enumerate(halves):
+        for step in range(1, tall_parts):
+            middle_terms[step - 1, :, lanes] = gathered(step, half)
+            second_copies.append(
                 remote(
-                    terms.at[near, tall_at[step]],
-                    beside_terms.at[step, near - 1],
-                    first_send.at[step, near - 1],
-                    first_recv.at[step, near - 1],
+                    middle_terms.at[step - 1, :, lanes],
+                    far_terms.at[step - 1, :, lanes],
+                    second_send.at[step - 1, half],
+                    second_recv.at[step - 1, half],
                     "vox",
-                    wide_peers[near],
+                    tall_peers[step],
                 )
             )
-    make_terms(0)
-
-    def gathered(step):
-        total = terms[0, tall_at[step]]
-        for near, copy in enumerate(first_copies[step]):
-            copy.wait_recv()
-            total = total + beside_terms[step, near]
-        return total
-
-    second_copies = []
-    for step in range(1, tall_parts):
-        middle_terms[step - 1] = gathered(step)
-        second_copies.append(
-            remote(
-                middle_terms.at[step - 1],
-                far_terms.at[step - 1],
-                second_send.at[step - 1],
-                second_recv.at[step - 1],
-                "vox",
-                tall_peers[step],
-            )
-        )
 
     share.wait_recv()
     smooth = spread_over_k(lambda k: smoothing[k])
@@ -337,10 +340,11 @@
         base[block] = smooth * (near_count * here - around)
 
     swap.wait_send()
-    total = gathered(0)
-    for copy_index, copy in enumerate(second_copies):
+    total = jnp.concatenate([gathered(0, 0), gathered(0, 1)], axis=1)
+    for copy in second_copies:
         copy.wait_recv()
-        total = total + far_terms[copy_index]
+    for step in range(1, tall_parts):
+        total = total + far_terms[step - 1]
     for k in range(k_count):
         partial[k * blocks_here : (k + 1) * blocks_here, :] = total[:, k * TILE : (k + 1) * TILE]
     for block in range(blocks_here):
@@ -439,10 +443,10 @@
             dma((tall_parts, wide_parts - 1)),
             dma((2,)),
             dma((2,)),
-            dma((tall_parts, wide_parts - 1)),
-            dma((tall_parts, wide_parts - 1)),
-            dma((tall_parts - 1,)),
-            dma((tall_parts - 1,)),
+            dma((tall_parts, wide_parts - 1, 2)),
+            dma((tall_parts, wide_parts - 1, 2)),
+            dma((tall_parts - 1, 2)),
+            dma((tall_parts - 1, 2)),
         ],
         compiler_params=pltpu.CompilerParams(
             collective_id=0, has_side_effects=True, vmem_limit_bytes=40 * 1024 * 1024

time: 31.3 us -> 30.7 us (0.981)
  Pallas kernels: 28.5 us -> 28 us
    pallas_call x1, Pallas kernels: 28.5 us -> 28 us  [local(): pl.pallas_call(functools.partial(kernel, wide_parts, tall_parts, groups),...]
where the time goes in v5:
time: 30.7 us; the launch traced here: 30.6 us
  Pallas kernels  28 us (91%)
  local copies, waits for them, and re-layouts  1.29 us (4%)
  between operations  1.29 us (4%)
    pallas_call x1, Pallas kernels, local(): pl.pallas_call(functools.partial(kernel, wide_parts, tall_parts, groups),...  28 us
    unnamed x2, local copies, waits for them, and re-layouts  1.29 us

profile of v5, /device:TPU:1, one launch (start us, length us, event | category | flops | bytes accessed | tf_op | source)
XLA Modules:
  0.0 30.6 jit_solution(10028482881406952235)
XLA Ops:
  1.3 28.0 %shard_map.113 = (f32[8,4096]{1,0:T(8,128)S(1)}, f32[8,1,2048]{2,1,0:T(1,128)S(1)}) custom-call(f32[8,1,2048]{2,1,0:T(1,128)} %fluence_in.1, f32[1,1,32,128,128]{4,3,2,1,0:T(8,128)} %values.1, s32[1,1,32]{2,1,0:T(1,128)} %row_in.1, s32[1,1,32]{2,1,0:T(1,128)} %column_in.1, s32[1,1]{1,0:T(1,128)S(6)} %copy.14.count_in, s32[32,128]{1,0:T(8,128)} %bitcast.3, ...), custom_call_target="tpu_custom_call" | custom-call | tf_op jit(solution)/shard_map/pallas_call | solution.py:403
  29.3 0.7 %copy.15 = f32[8,4096]{1,0:T(8,128)} copy(f32[8,4096]{1,0:T(8,128)S(1)} %get-tuple-element.4) | data formatting | bytes 262144
  29.9 0.6 %copy.16 = f32[8,1,2048]{2,1,0:T(1,128)} copy(f32[8,1,2048]{2,1,0:T(1,128)S(1)} %get-tuple-element.5) | data formatting | bytes 131072

commit v6 on v5

--- a/solution.py
+++ b/solution.py
@@ -281,8 +281,8 @@
             terms[near, part] = found[part * blocks_here : (part + 1) * blocks_here, :]
 
     steps = list(range(1, tall_parts)) + [0]
-    halves = [pl.ds(half * (k_count // 2) * TILE, k_count // 2 * TILE) for half in range(2)]
-    first_copies = {(step, half): [] for step in steps for half in range(2)}
+    halves = [pl.ds(half * (k_count // 4) * TILE, k_count // 4 * TILE) for half in range(4)]
+    first_copies = {(step, half): [] for step in steps for half in range(4)}
     for near in range(1, wide_parts):
         make_terms(near)
         for half, lanes in enumerate(halves):
@@ -340,7 +340,7 @@
         base[block] = smooth * (near_count * here - around)
 
     swap.wait_send()
-    total = jnp.concatenate([gathered(0, 0), gathered(0, 1)], axis=1)
+    total = jnp.concatenate([gathered(0, half) for half in range(4)], axis=1)
     for copy in second_copies:
         copy.wait_recv()
     for step in range(1, tall_parts):
@@ -443,10 +443,10 @@
             dma((tall_parts, wide_parts - 1)),
             dma((2,)),
             dma((2,)),
-            dma((tall_parts, wide_parts - 1, 2)),
-            dma((tall_parts, wide_parts - 1, 2)),
-            dma((tall_parts - 1, 2)),
-            dma((tall_parts - 1, 2)),
+            dma((tall_parts, wide_parts - 1, 4)),
+            dma((tall_parts, wide_parts - 1, 4)),
+            dma((tall_parts - 1, 4)),
+            dma((tall_parts - 1, 4)),
         ],
         compiler_params=pltpu.CompilerParams(
             collective_id=0, has_side_effects=True, vmem_limit_bytes=40 * 1024 * 1024

time: 30.7 us -> 31.7 us (1.033)
  Pallas kernels: 28 us -> 28.8 us
    pallas_call x1, Pallas kernels: 28 us -> 28.8 us  [local(): pl.pallas_call(functools.partial(kernel, wide_parts, tall_parts, groups),...]
where the time goes in v6:
time: 31.7 us; the launch traced here: 31.4 us
  Pallas kernels  28.8 us (91%)
  local copies, waits for them, and re-layouts  1.29 us (4%)
  between operations  1.29 us (4%)
    pallas_call x1, Pallas kernels, local(): pl.pallas_call(functools.partial(kernel, wide_parts, tall_parts, groups),...  28.8 us
    unnamed x2, local copies, waits for them, and re-layouts  1.29 us

profile of v6, /device:TPU:1, one launch (start us, length us, event | category | flops | bytes accessed | tf_op | source)
XLA Modules:
  0.0 31.4 jit_solution(14440423219792577811)
XLA Ops:
  1.3 28.8 %shard_map.113 = (f32[8,4096]{1,0:T(8,128)S(1)}, f32[8,1,2048]{2,1,0:T(1,128)S(1)}) custom-call(f32[8,1,2048]{2,1,0:T(1,128)} %fluence_in.1, f32[1,1,32,128,128]{4,3,2,1,0:T(8,128)} %values.1, s32[1,1,32]{2,1,0:T(1,128)} %row_in.1, s32[1,1,32]{2,1,0:T(1,128)} %column_in.1, s32[1,1]{1,0:T(1,128)S(6)} %copy.14.count_in, s32[32,128]{1,0:T(8,128)} %bitcast.3, ...), custom_call_target="tpu_custom_call" | custom-call | tf_op jit(solution)/shard_map/pallas_call | solution.py:403
  30.1 0.7 %copy.15 = f32[8,4096]{1,0:T(8,128)} copy(f32[8,4096]{1,0:T(8,128)S(1)} %get-tuple-element.4) | data formatting | bytes 262144
  30.7 0.6 %copy.16 = f32[8,1,2048]{2,1,0:T(1,128)} copy(f32[8,1,2048]{2,1,0:T(1,128)S(1)} %get-tuple-element.5) | data formatting | bytes 131072
